TPU v7x, 32 devices: a whole 2x2x4 slice. The times are simulated.
32 devices in a mesh: section: 2 (over x), dp: 16 (over z, y, core).
Axes of the slice: x: 2, y: 2, z: 4, core: 2. Of those that a mesh axis runs over, the one named last changes fastest.
Arguments:
- boundary: bfloat16 [2, 16384, 768], P('section', 'dp'), may hold values from -6 to 6
- inward: bfloat16 [2, 768, 2304], P('section'), may hold values from -0.21875 to 0.21875
- inbias: float32 [2, 2304], P('section'), may hold values from -1.5 to 1.5
- outward: bfloat16 [2, 768, 768], P('section'), may hold values from -3 to 3
- outbias: float32 [2, 768], P('section'), may hold values from -1.5 to 1.5
- normgain: float32 [2, 768], P('section'), may hold values from 0.25 to 1.75
- normshift: float32 [2, 768], P('section'), may hold values from -1.5 to 1.5
- expand: bfloat16 [2, 768, 3072], P('section'), may hold values from -0.21875 to 0.21875
- expbias: float32 [2, 3072], P('section'), may hold values from -1.5 to 1.5
- shrink: bfloat16 [2, 3072, 768], P('section'), may hold values from -0.109375 to 0.109375
- shrbias: float32 [2, 768], P('section'), may hold values from -1.5 to 1.5
- lastgain: float32 [2, 768], P('section'), may hold values from 0.25 to 1.75
- lastshift: float32 [2, 768], P('section'), may hold values from -1.5 to 1.5
Outputs:
- results: bfloat16 [2, 16384, 768], P('section', 'dp')
- inward_grads: float32 [2, 768, 2304], P('section')
- inbias_grads: float32 [2, 2304], P('section')
- outward_grads: float32 [2, 768, 768], P('section')
- outbias_grads: float32 [2, 768], P('section')
- normgain_grads: float32 [2, 768], P('section')
- normshift_grads: float32 [2, 768], P('section')
- expand_grads: float32 [2, 768, 3072], P('section')
- expbias_grads: float32 [2, 3072], P('section')
- shrink_grads: float32 [2, 3072, 768], P('section')
- shrbias_grads: float32 [2, 768], P('section')
- lastgain_grads: float32 [2, 768], P('section')
- lastshift_grads: float32 [2, 768], P('section')
All inputs are finite; a program needn't handle non-finite values.
Results may differ from a plain program's by a relative error of at most 0.014.
Values may be sent and summed in bfloat16 or wider, within the bound.
A program may use at most 384 MiB of HBM per device.

v0:
```python
from functools import partial
import math

import jax
import jax.numpy as jnp
from jax import lax
from jax.sharding import PartitionSpec as P

HEAD = 64
SEQ = 512
MICRO = 2
SEQ_MB = 1


EPSILON = 1e-05
PRECISE = lax.Precision.HIGHEST


def passed_along(array, axis, by):
    count = lax.axis_size(axis)
    pairs = [(i, i + by) for i in range(count) if 0 <= i + by < count]
    return lax.ppermute(array, axis, pairs)


def shortened(array):

    def short(part):
        return part.astype(jnp.bfloat16) if part.dtype == jnp.float32 else part

    return jax.tree.map(short, array)


def product(operand, matrix):
    return jnp.dot(operand, matrix, preferred_element_type=jnp.float32)


def over_rows(former, latter):
    return lax.dot_general(
        former, latter, (((0,), (0,)), ((), ())), preferred_element_type=jnp.float32
    )


def against(operand, matrix):
    return lax.dot_general(
        operand, matrix, (((1,), (1,)), ((), ())), preferred_element_type=jnp.float32
    )


def column_sum(operand):
    return jnp.sum(operand, axis=0, dtype=jnp.float32)


def layer_norm(values, norm_gain, norm_shift):
    center = values - jnp.mean(values, axis=-1, keepdims=True)
    spread = jnp.mean(center * center, axis=-1, keepdims=True)
    return center * lax.rsqrt(spread + EPSILON) * norm_gain + norm_shift


def attention(queries, keys_in, values_in, block_width):
    seq_count, seq_length, head_count, head_size = queries.shape
    block_count = seq_length // block_width
    angle_step = math.pi / (2.0 * seq_length)
    angles = (
        jnp.arange(seq_length).astype(jnp.float32).reshape(block_count, block_width) * angle_step
    )
    causal = jnp.arange(block_width)[:, None] >= jnp.arange(block_width)[None, :]

    def split_blocks(source):
        return jnp.moveaxis(
            source.reshape(seq_count, block_count, block_width, head_count, head_size), 1, 0
        )

    def block_step(carried, inputs):
        cosine_state, sine_state, cosine_norm, sine_norm = carried
        query_block, key_block, value_block, block_angles = inputs
        cosine_factor = jnp.cos(block_angles)[None, :, None, None]
        sine_factor = jnp.sin(block_angles)[None, :, None, None]
        weighting = jnp.where(causal, jnp.cos(block_angles[:, None] - block_angles[None, :]), 0.0)
        scores = (
            jnp.einsum("bihe,bjhe->bhij", query_block, key_block, precision=PRECISE) * weighting
        )
        query_cosine = query_block * cosine_factor
        query_sine = query_block * sine_factor
        numerator = jnp.einsum("bhij,bjhe->bihe", scores, value_block, precision=PRECISE)
        numerator = numerator + jnp.einsum(
            "bihe,bhef->bihf", query_cosine, cosine_state, precision=PRECISE
        )
        numerator = numerator + jnp.einsum(
            "bihe,bhef->bihf", query_sine, sine_state, precision=PRECISE
        )
        denominator = jnp.transpose(jnp.sum(scores, axis=-1), (0, 2, 1))
        denominator = denominator + jnp.einsum(
            "bihe,bhe->bih", query_cosine, cosine_norm, precision=PRECISE
        )
        denominator = denominator + jnp.einsum(
            "bihe,bhe->bih", query_sine, sine_norm, precision=PRECISE
        )
        key_cosine = key_block * cosine_factor
        key_sine = key_block * sine_factor
        cosine_state = cosine_state + jnp.einsum(
            "bjhe,bjhf->bhef", key_cosine, value_block, precision=PRECISE
        )
        sine_state = sine_state + jnp.einsum(
            "bjhe,bjhf->bhef", key_sine, value_block, precision=PRECISE
        )
        cosine_norm = cosine_norm + jnp.sum(key_cosine, axis=1)
        sine_norm = sine_norm + jnp.sum(key_sine, axis=1)
        return (
            (cosine_state, sine_state, cosine_norm, sine_norm),
            numerator / denominator[..., None],
        )

    initial = (
        jnp.zeros((seq_count, head_count, head_size, head_size), jnp.float32),
        jnp.zeros((seq_count, head_count, head_size, head_size), jnp.float32),
        jnp.zeros((seq_count, head_count, head_size), jnp.float32),
        jnp.zeros((seq_count, head_count, head_size), jnp.float32),
    )
    unused_state, blocks_out = lax.scan(
        jax.checkpoint(block_step),
        initial,
        (split_blocks(queries), split_blocks(keys_in), split_blocks(values_in), angles),
    )
    return jnp.moveaxis(blocks_out, 0, 1).reshape(seq_count, seq_length, head_count, head_size)


def attend_float(queries, keys_in, values_in):
    row_count, model_width = queries.shape
    shape_four = (row_count // SEQ, SEQ, model_width // HEAD, HEAD)
    result = attention(
        queries.reshape(shape_four),
        keys_in.reshape(shape_four),
        values_in.reshape(shape_four),
        min(64, SEQ // 4),
    )
    return result.reshape(row_count, model_width)


def forward(layer_input, params):
    (
        inward,
        inbias,
        outward,
        outbias,
        normgain,
        normshift,
        expand,
        expbias,
        shrink,
        shrbias,
        lastgain,
        lastshift,
    ) = params
    model_width = layer_input.shape[1]
    packed = product(layer_input, inward) + inbias
    queries = jax.nn.softplus(packed[:, :model_width]).astype(jnp.bfloat16)
    keys_in = jax.nn.softplus(packed[:, model_width : 2 * model_width]).astype(jnp.bfloat16)
    values_in = packed[:, 2 * model_width :].astype(jnp.bfloat16)
    attended = attend_float(
        queries.astype(jnp.float32), keys_in.astype(jnp.float32), values_in.astype(jnp.float32)
    ).astype(jnp.bfloat16)
    before = layer_input.astype(jnp.float32) + (product(attended, outward) + outbias)
    hidden = layer_norm(before, normgain, normshift)
    hidden_low = hidden.astype(jnp.bfloat16)
    lifted = product(hidden_low, expand) + expbias
    active = jax.nn.gelu(lifted, approximate=False).astype(jnp.bfloat16)
    summed = hidden + (product(active, shrink) + shrbias)
    output = layer_norm(summed, lastgain, lastshift).astype(jnp.bfloat16)
    compact = (layer_input, queries, keys_in, values_in, attended, hidden_low, active)
    return (output, compact)


def complete(compact, params):
    (
        inward,
        inbias,
        outward,
        outbias,
        normgain,
        normshift,
        expand,
        expbias,
        shrink,
        shrbias,
        lastgain,
        lastshift,
    ) = params
    layer_input, queries, keys_in, values_in, attended, hidden_low, active = compact
    packed = product(layer_input, inward) + inbias
    before = layer_input.astype(jnp.float32) + (product(attended, outward) + outbias)
    hidden = layer_norm(before, normgain, normshift)
    lifted = product(hidden_low, expand) + expbias
    summed = hidden + (product(active, shrink) + shrbias)
    return (
        layer_input,
        packed,
        queries,
        keys_in,
        values_in,
        attended,
        before,
        hidden_low,
        lifted,
        active,
        summed,
    )


def backward_inputs(incoming, retained, params):
    (
        inward,
        inbias,
        outward,
        outbias,
        normgain,
        normshift,
        expand,
        expbias,
        shrink,
        shrbias,
        lastgain,
        lastshift,
    ) = params
    (
        layer_input,
        packed,
        queries,
        keys_in,
        values_in,
        attended,
        before,
        hidden_low,
        lifted,
        active,
        summed,
    ) = retained
    model_width = layer_input.shape[1]
    unused_out, last_pull = jax.vjp(layer_norm, summed, lastgain, lastshift)
    summed_grad, lastgain_grad, lastshift_grad = last_pull(incoming.astype(jnp.float32))
    reduced_low = summed_grad.astype(jnp.bfloat16)
    active_grad = against(reduced_low, shrink)
    unused_out, gelu_pull = jax.vjp(partial(jax.nn.gelu, approximate=False), lifted)
    lifted_low = gelu_pull(active_grad)[0].astype(jnp.bfloat16)
    hidden_grad = summed_grad + against(lifted_low, expand)
    unused_out, first_pull = jax.vjp(layer_norm, before, normgain, normshift)
    before_grad, normgain_grad, normshift_grad = first_pull(hidden_grad)
    branch_low = before_grad.astype(jnp.bfloat16)
    attended_low = lax.optimization_barrier(against(branch_low, outward).astype(jnp.bfloat16))
    unused_out, attend_pull = jax.vjp(
        attend_float,
        queries.astype(jnp.float32),
        keys_in.astype(jnp.float32),
        values_in.astype(jnp.float32),
    )
    query_grad, key_grad, value_grad = attend_pull(attended_low.astype(jnp.float32))
    packed_low = jnp.concatenate(
        [
            query_grad * jax.nn.sigmoid(packed[:, :model_width]),
            key_grad * jax.nn.sigmoid(packed[:, model_width : 2 * model_width]),
            value_grad,
        ],
        axis=1,
    ).astype(jnp.bfloat16)
    input_grad = (before_grad + against(packed_low, inward)).astype(jnp.bfloat16)
    pending = (
        layer_input,
        packed_low,
        attended,
        branch_low,
        hidden_low,
        lifted_low,
        active,
        reduced_low,
    )
    vectors = (
        column_sum(packed_low),
        column_sum(branch_low),
        normgain_grad,
        normshift_grad,
        column_sum(lifted_low),
        column_sum(reduced_low),
        lastgain_grad,
        lastshift_grad,
    )
    return (input_grad, pending, vectors)


def backward_weights(pending):
    layer_input, packed_low, attended, branch_low, hidden_low, lifted_low, active, reduced_low = (
        pending
    )
    return (
        over_rows(layer_input, packed_low),
        over_rows(attended, branch_low),
        over_rows(hidden_low, lifted_low),
        over_rows(active, reduced_low),
    )


def arrange(matrices, vectors):
    return (
        matrices[0],
        vectors[0],
        matrices[1],
        vectors[1],
        vectors[2],
        vectors[3],
        matrices[2],
        vectors[4],
        matrices[3],
        vectors[5],
        vectors[6],
        vectors[7],
    )


def blank_rows(row_count, columns, kind):
    return jnp.zeros((row_count, columns), kind)


def blank_vectors(model_width, hidden_width):
    sizes_list = (
        3 * model_width,
        model_width,
        model_width,
        model_width,
        hidden_width,
        model_width,
        model_width,
        model_width,
    )
    return tuple((jnp.zeros((length_one,), jnp.float32) for length_one in sizes_list))


def blank_inputs(row_count, model_width, hidden_width):
    low_type = jnp.bfloat16
    pending = (
        blank_rows(row_count, model_width, low_type),
        blank_rows(row_count, 3 * model_width, low_type),
        blank_rows(row_count, model_width, low_type),
        blank_rows(row_count, model_width, low_type),
        blank_rows(row_count, model_width, low_type),
        blank_rows(row_count, hidden_width, low_type),
        blank_rows(row_count, hidden_width, low_type),
        blank_rows(row_count, model_width, low_type),
    )
    return (
        blank_rows(row_count, model_width, low_type),
        pending,
        blank_vectors(model_width, hidden_width),
    )


def blank_weights(model_width, hidden_width):
    return (
        jnp.zeros((model_width, 3 * model_width), jnp.float32),
        jnp.zeros((model_width, model_width), jnp.float32),
        jnp.zeros((model_width, hidden_width), jnp.float32),
        jnp.zeros((hidden_width, model_width), jnp.float32),
    )


def shards(
    boundary,
    inward,
    inbias,
    outward,
    outbias,
    normgain,
    normshift,
    expand,
    expbias,
    shrink,
    shrbias,
    lastgain,
    lastshift,
):
    params = tuple(
        (
            weight[0]
            for weight in (
                inward,
                inbias,
                outward,
                outbias,
                normgain,
                normshift,
                expand,
                expbias,
                shrink,
                shrbias,
                lastgain,
                lastshift,
            )
        )
    )
    section_index = lax.axis_index("section")
    first_section = section_index == 0
    own_slab = boundary[0]
    model_width = own_slab.shape[1]
    hidden_width = params[6].shape[1]
    row_count = SEQ_MB * SEQ
    blank_entry = jnp.zeros((row_count, model_width), jnp.bfloat16)
    widths = (model_width,) * 6 + (hidden_width,)
    saved_buffer = tuple(
        (jnp.zeros((MICRO, row_count, width_one), jnp.bfloat16) for width_one in widths)
    )

    def run_forward(layer_input, buffer, slot):
        output, compact = forward(layer_input, params)
        buffer = tuple(
            (
                lax.dynamic_update_index_in_dim(whole, piece, slot, 0)
                for whole, piece in zip(buffer, compact)
            )
        )
        return (output, buffer)

    def skip_forward(layer_input, buffer, slot):
        return (blank_entry, buffer)

    def restore(compact):
        return complete(compact, params)

    def run_inputs(incoming, compact):
        return backward_inputs(incoming, restore(compact), params)

    def skip_inputs(incoming, compact):
        return blank_inputs(row_count, model_width, hidden_width)

    def skip_weights(pending):
        return blank_weights(model_width, hidden_width)

    def collect(accumulated, matrices, vectors):
        gradients = arrange(matrices, vectors)
        return tuple((earlier_sum + added for earlier_sum, added in zip(accumulated, gradients)))

    outputs = []
    arriving = blank_entry
    for moment in range(MICRO + 1):
        batch_index = moment - section_index
        is_valid = jnp.logical_and(batch_index >= 0, batch_index < MICRO)
        slot = jnp.clip(batch_index, 0, MICRO - 1)
        own_rows = (
            own_slab[moment * row_count : (moment + 1) * row_count]
            if moment < MICRO
            else blank_entry
        )
        layer_input = jnp.where(first_section, own_rows, arriving)
        output, saved_buffer = lax.cond(
            is_valid, run_forward, skip_forward, layer_input, saved_buffer, slot
        )
        outputs.append(output)
        if moment < MICRO:
            arriving = passed_along(output, "section", 1)
    divisor = 1
    accumulated = tuple(
        (jnp.zeros((param.shape[0] // divisor,) + param.shape[1:], jnp.float32) for param in params)
    )
    returning = blank_entry
    input_grads = []
    for moment in range(MICRO + 1):
        batch_index = moment - 1 + section_index
        is_valid = jnp.logical_and(batch_index >= 0, batch_index < MICRO)
        slot = jnp.clip(batch_index, 0, MICRO - 1)
        own_rows = (
            own_slab[moment * row_count : (moment + 1) * row_count]
            if moment < MICRO
            else blank_entry
        )
        incoming = jnp.where(first_section, returning, own_rows)
        compact = tuple(
            (lax.dynamic_index_in_dim(whole, slot, 0, keepdims=False) for whole in saved_buffer)
        )
        input_grad, pending, vectors = lax.cond(
            is_valid, run_inputs, skip_inputs, incoming, compact
        )
        if moment < MICRO:
            returning = passed_along(input_grad, "section", -1)
        if moment > 0:
            matrices = lax.cond(waiting_valid, backward_weights, skip_weights, waiting)
            accumulated = collect(accumulated, matrices, waiting_vectors)
        waiting, waiting_valid, waiting_vectors = (pending, is_valid, vectors)
        input_grads.append(input_grad)
    matrices = lax.cond(waiting_valid, backward_weights, skip_weights, waiting)
    accumulated = collect(accumulated, matrices, waiting_vectors)
    accumulated = lax.psum_scatter(accumulated, "dp", scatter_dimension=0, tiled=True)
    gathered = jax.tree.map(
        lambda part, own: part.astype(own.dtype),
        lax.all_gather(shortened(accumulated), "dp", axis=0, tiled=True),
        accumulated,
    )
    pieces = [
        jnp.where(first_section, input_grads[moment + 1], outputs[moment + 1])
        for moment in range(MICRO)
    ]
    results = jnp.concatenate(pieces, axis=0)[None]
    return (results,) + tuple((element[None] for element in gathered))


def solution(mesh):
    in_specs = (
        P("section", "dp", None),
        P("section", None, None),
        P("section", None),
        P("section", None, None),
        P("section", None),
        P("section", None),
        P("section", None),
        P("section", None, None),
        P("section", None),
        P("section", None, None),
        P("section", None),
        P("section", None),
        P("section", None),
    )
    out_specs = (
        P("section", "dp", None),
        P("section", None, None),
        P("section", None),
        P("section", None, None),
        P("section", None),
        P("section", None),
        P("section", None),
        P("section", None, None),
        P("section", None),
        P("section", None, None),
        P("section", None),
        P("section", None),
        P("section", None),
    )
    return jax.shard_map(shards, mesh=mesh, in_specs=in_specs, out_specs=out_specs, check_vma=False)
```

profile of v0, /device:TPU:0, one launch (start us, length us, event | category | flops | bytes accessed | tf_op | source)
XLA Modules:
  0.0 2687.6 jit_solution(14747068229451125707)
XLA Ops:
  11.1 217.4 %conditional.9 = (bf16[512,768]{1,0:T(8,128)(2,1)}, bf16[2,512,768]{2,1,0:T(8,128)(2,1)}, bf16[2,512,768]{2,1,0:T(8,128)(2,1)}, bf16[2,512,768]{2,1,0:T(8,128)(2...) conditional(s32[]{:T(128)} %convert_element_type.523, ...), branch_computations={%region_0.1_spmd, %region_1.11_spmd} | conditional | flops 7606633984 | bytes 148853552 | solution.py:450
  57.7 127.2 %while.240 = (s32[]{:T(128)}, f32[1,12,64,64]{3,2,1,0:T(8,128)}, f32[1,12,64,64]{3,2,1,0:T(8,128)S(1)}, f32[1,12,64]{2,1,0:T(8,128)}, f32[1,12,64]{2,1,0:T(8,128...) while((s32[]{:T(128)}, f32[1,12,64,64]{3,2,1,0:T(8,128)}, ...), condition=%wide.region_6.6_spmd.clone, body=%wide.region_2.5_spmd.clone.sunk | while | flops 228718848 | bytes 9770200 | solution.py:119
  204.9 18.9 bitcast_dynamic-update-slice_fusion.12
  247.8 205.0 %conditional.10 = (bf16[512,768]{1,0:T(8,128)(2,1)}, bf16[2,512,768]{2,1,0:T(8,128)(2,1)}, bf16[2,512,768]{2,1,0:T(8,128)(2,1)}, bf16[2,512,768]{2,1,0:T(8,128)(...) conditional(s32[]{:T(128)} %convert_element_type.522, ...), branch_computations={%region_11.12_spmd, %region_12.22_spmd} | conditional | flops 7606633984 | bytes 203903968 | solution.py:450
  289.7 127.1 %while.241 = (s32[]{:T(128)}, f32[1,12,64,64]{3,2,1,0:T(8,128)}, f32[1,12,64,64]{3,2,1,0:T(8,128)S(1)}, f32[1,12,64]{2,1,0:T(8,128)}, f32[1,12,64]{2,1,0:T(8,128...) while((s32[]{:T(128)}, f32[1,12,64,64]{3,2,1,0:T(8,128)}, ...), condition=%wide.region_17.17_spmd.clone, body=%wide.region_13.16_spmd.clone.sunk | while | flops 228718848 | bytes 9770200 | solution.py:119
  483.8 24.2 conditional.12
  509.3 623.0 %collective-permute-done.2 = bf16[512,768]{1,0:T(8,128)(2,1)S(1)} collective-permute-done((bf16[512,768]{1,0:T(8,128)(2,1)}, bf16[512,768]{1,0:T(8,128)(2,1)S(1)}, u32[]{:S(2)}, u32[]{:S(2)}) %collective-permute-start.2) | collective-permute-done | bytes 786464 | tf_op jit(solution)/shard_map/ppermute | solution.py:22
  1132.4 437.4 %conditional.13 = (bf16[512,768]{1,0:T(8,128)(2,1)}, bf16[512,768]{1,0:T(8,128)(2,1)}, bf16[512,2304]{1,0:T(8,128)(2,1)}, bf16[512,768]{1,0:T(8,128)(2,1)}, bf16...) conditional(s32[]{:T(128)} %convert_element_type.519, ...), branch_computations={%region_59.60_spmd, %region_60.85_spmd} | conditional | flops 15339425792 | bytes 320323104 | solution.py:475
  1182.7 64.3 %while.245 = (s32[]{:T(128)}, f32[1,12,64,64]{3,2,1,0:T(8,128)S(1)}, f32[1,12,64,64]{3,2,1,0:T(8,128)S(1)}, f32[1,12,64]{2,1,0:T(8,128)S(1)}, f32[1,12,64]{2,1,0...) while((s32[]{:T(128)}, f32[1,12,64,64]{3,2,1,0:T(8,128)S(1)}, ...), condition=%wide.region_72.72_spmd.clone, body=%wide.region_69.71_spmd.clone.sunk | while | flops 76090368 | bytes 3784627 | solution.py:119
  1258.4 21.5 convert_reduce_fusion.5
  1303.0 231.6 %while.246 = (s32[]{:T(128)}, f32[1,12,64,64]{2,3,1,0:T(8,128)S(1)}, f32[1,12,64,64]{2,3,1,0:T(8,128)S(1)}, f32[1,12,64]{2,1,0:T(8,128)S(1)}, f32[1,12,64]{2,1,0...) while((s32[]{:T(128)}, f32[1,12,64,64]{2,3,1,0:T(8,128)S(1)}, ...), condition=%wide.region_76.76_spmd.clone, body=%wide.region_73.75_spmd.clone.sunk | while | flops 608568576 | bytes 17007064 | solution.py:119
  1583.3 23.0 conditional.16
  1610.0 445.2 %conditional.14 = (bf16[512,768]{1,0:T(8,128)(2,1)}, bf16[512,768]{1,0:T(8,128)(2,1)S(1)}, bf16[512,2304]{1,0:T(8,128)(2,1)}, bf16[512,768]{1,0:T(8,128)(2,1)S(1...) conditional(s32[]{:T(128)} %convert_element_type.524, ...), branch_computations={%region_85.86_spmd, %region_86.111_spmd} | conditional | flops 15339425792 | bytes 334614496 | solution.py:475
  1664.6 64.4 %while.247 = (s32[]{:T(128)}, f32[1,12,64,64]{3,2,1,0:T(8,128)S(1)}, f32[1,12,64,64]{3,2,1,0:T(8,128)S(1)}, f32[1,12,64]{2,1,0:T(8,128)S(1)}, f32[1,12,64]{2,1,0...) while((s32[]{:T(128)}, f32[1,12,64,64]{3,2,1,0:T(8,128)S(1)}, ...), condition=%wide.region_98.98_spmd.clone, body=%wide.region_95.97_spmd.clone.sunk | while | flops 76090368 | bytes 3784627 | solution.py:119
  1740.4 20.2 convert_reduce_fusion.10
  1783.8 236.4 %while.248 = (s32[]{:T(128)}, f32[1,12,64,64]{2,3,1,0:T(8,128)S(1)}, f32[1,12,64,64]{2,3,1,0:T(8,128)S(1)}, f32[1,12,64]{2,1,0:T(8,128)}, f32[1,12,64]{2,1,0:T(8...) while((s32[]{:T(128)}, f32[1,12,64,64]{2,3,1,0:T(8,128)S(1)}, ...), condition=%wide.region_102.102_spmd.clone, body=%wide.region_99.101_spmd.clone.sunk | while | flops 608568576 | bytes 16982432 | solution.py:119
  2056.3 24.6 conditional.17
  2126.2 21.3 reduce-scatter.7.cloned.1.call-done
  2149.0 92.6 %reduce-scatter.5.cloned.1.call-done = f32[48,2304]{1,0:T(8,128)} async-done(((f32[768,2304]{1,0:T(8,128)}), f32[48,2304]{1,0:T(8,128)}) %reduce-scatter.5.cloned.1.call-update) | async-done | bytes 442384 | tf_op jit(solution)/shard_map/reduce_scatter | solution.py:487
  2243.4 113.8 %reduce-scatter.11.cloned.1.call-done = f32[192,768]{1,0:T(8,128)} async-done(((f32[3072,768]{1,0:T(8,128)}), f32[192,768]{1,0:T(8,128)}) %reduce-scatter.11.cloned.1.call-update) | async-done | bytes 589840 | tf_op jit(solution)/shard_map/reduce_scatter | solution.py:487
  2359.1 114.3 %reduce-scatter.9.cloned.1.call-done = f32[48,3072]{1,0:T(8,128)} async-done(((f32[768,3072]{1,0:T(8,128)}), f32[48,3072]{1,0:T(8,128)}) %reduce-scatter.9.cloned.1.call-update) | async-done | bytes 589840 | tf_op jit(solution)/shard_map/reduce_scatter | solution.py:487
  2484.6 61.0 %all-reduce.16 = (bf16[2304]{0:T(1024)(128)(2,1)S(1)}, bf16[768]{0:T(1024)(128)(2,1)S(1)}, bf16[768]{0:T(1024)(128)(2,1)S(1)}, bf16[768]{0:T(1024)(128)(2,1)S(1)...) all-reduce(f32[2304]{0:T(1024)S(1)} %add_add_fusion.26, ...), channel_id=3, replica_groups=mesh['section'=2,'dp'=16] {'dp'}, use_global_device_ids=true, to_apply=%region_118.119.clone | all-reduce | flops 9984 | bytes 59904
  2547.9 58.9 %all-reduce.17 = (bf16[2304]{0:T(1024)(128)(2,1)S(1)}, bf16[768]{0:T(1024)(128)(2,1)S(1)}, bf16[768]{0:T(1024)(128)(2,1)S(1)}, bf16[768]{0:T(1024)(128)(2,1)S(1)...) all-reduce(bf16[2304]{0:T(1024)(128)(2,1)S(1)} %dynamic-update-slic, ...), channel_id=1, replica_groups=mesh['section'=2,'dp'=16] {'dp'}, use_global_device_ids=true, to_apply=%add | all-reduce | flops 9984 | bytes 39936
  2629.1 44.0 %all-gather.9.cloned.1.call-done = bf16[768,3072]{1,0:T(8,128)(2,1)} async-done(((bf16[48,3072]{1,0:T(8,128)(2,1)}), bf16[768,3072]{1,0:T(8,128)(2,1)}) %all-gather.9.cloned.1.call-update) | async-done | bytes 4718608 | tf_op jit(solution)/shard_map/all_gather | solution.py:490
  (1847 shorter events, 1464.4 us)
Async XLA Ops:
  7.3 2140.2 %reduce-scatter.7.cloned.1.call-start = ((), (), s32[]{:S(2)}) async-start(), calls=%async_computation.6 | async-start | bytes 2506752 | tf_op jit(solution)/shard_map/reduce_scatter | solution.py:487
  228.5 19.3 collective-permute-start
  452.8 21.4 collective-permute-start.1
  508.0 624.3 %collective-permute-start.2 = (bf16[512,768]{1,0:T(8,128)(2,1)}, bf16[512,768]{1,0:T(8,128)(2,1)S(1)}, u32[]{:S(2)}, u32[]{:S(2)}) collective-permute-start(bf16[512,768]{1,0:T(8,128)(2,1)} %get-tuple-element.2583), channel_id=1, source_target_pairs={{16,0},{17,1},{18,2},{19,3},{20,4},{21,5},{22,6},{23,7},{24,8},{25... | collective-permute-start | bytes 2359304 | tf_op jit(solution)/shard_map/ppermute | solution.py:22
  1569.8 36.5 %collective-permute-start.3 = (bf16[512,768]{1,0:T(8,128)(2,1)}, bf16[512,768]{1,0:T(8,128)(2,1)S(1)}, u32[]{:S(2)}, u32[]{:S(2)}) collective-permute-start(bf16[512,768]{1,0:T(8,128)(2,1)} %get-tuple-element.2584), channel_id=1, source_target_pairs={{16,0},{17,1},{18,2},{19,3},{20,4},{21,5},{22,6},{23,7},{24,8},{25... | collective-permute-start | bytes 2359304 | tf_op jit(solution)/shard_map/ppermute | solution.py:22
  1574.0 32.4 %copy-start.5 = (bf16[512,768]{1,0:T(8,128)(2,1)S(1)}, bf16[512,768]{1,0:T(8,128)(2,1)}, u32[]{:S(2)}) copy-start(bf16[512,768]{1,0:T(8,128)(2,1)} %copy-done.4) | copy-start | bytes 2359300
  1664.6 64.4 %copy-start.64 = (bf16[512,768]{1,0:T(8,128)(2,1)S(1)}, bf16[512,768]{1,0:T(8,128)(2,1)}, u32[]{:S(2)}) copy-start(bf16[512,768]{1,0:T(8,128)(2,1)} %copy-done.63) | copy-start | bytes 2359300 | tf_op jit(solution)/shard_map/cond
  1664.6 64.4 %copy-start.147 = (f32[2304]{0:T(1024)S(1)}, f32[2304]{0:T(1024)}, u32[]{:S(2)}) copy-start(f32[2304]{0:T(1024)} %reduce.101) | copy-start | bytes 27652 | tf_op jit(solution)/shard_map/cond
  2084.4 157.2 %reduce-scatter.5.cloned.1.call-start = ((), (), s32[]{:S(2)}) async-start(), calls=%async_computation.4 | async-start | bytes 7520256 | tf_op jit(solution)/shard_map/reduce_scatter | solution.py:487
  2095.9 261.3 %reduce-scatter.11.cloned.1.call-start = ((), (), s32[]{:S(2)}) async-start(), calls=%async_computation.10 | async-start | bytes 10027008 | tf_op jit(solution)/shard_map/reduce_scatter | solution.py:487
  2110.5 362.9 %reduce-scatter.9.cloned.1.call-start = ((), (), s32[]{:S(2)}) async-start(), calls=%async_computation.8 | async-start | bytes 10027008 | tf_op jit(solution)/shard_map/reduce_scatter | solution.py:487
  2126.0 349.2 %copy-start.165 = (u32[32]{0:T(128)S(1)}, u32[32]{0:T(128)}, u32[]{:S(2)}) copy-start(u32[32]{0:T(128)} %constant.1261) | copy-start | bytes 388
  2126.0 355.0 %copy-start.139 = (f32[768]{0:T(1024)S(1)}, f32[768]{0:T(1024)}, u32[]{:S(2)}) copy-start(f32[768]{0:T(1024)} %get-tuple-element.2646) | copy-start | bytes 9220
  2126.0 355.0 %copy-start.140 = (f32[768]{0:T(1024)S(1)}, f32[768]{0:T(1024)}, u32[]{:S(2)}) copy-start(f32[768]{0:T(1024)} %get-tuple-element.2643) | copy-start | bytes 9220
  2126.1 355.7 %copy-start.141 = (f32[768]{0:T(1024)S(1)}, f32[768]{0:T(1024)}, u32[]{:S(2)}) copy-start(f32[768]{0:T(1024)} %get-tuple-element.2640) | copy-start | bytes 9220
  2126.1 355.7 %copy-start.142 = (f32[768]{0:T(1024)S(1)}, f32[768]{0:T(1024)}, u32[]{:S(2)}) copy-start(f32[768]{0:T(1024)} %get-tuple-element.2628) | copy-start | bytes 9220
  2126.1 356.3 %copy-start.143 = (f32[768]{0:T(1024)S(1)}, f32[768]{0:T(1024)}, u32[]{:S(2)}) copy-start(f32[768]{0:T(1024)} %get-tuple-element.2625) | copy-start | bytes 9220
  2126.1 356.3 %copy-start.144 = (f32[768]{0:T(1024)S(1)}, f32[768]{0:T(1024)}, u32[]{:S(2)}) copy-start(f32[768]{0:T(1024)} %get-tuple-element.2622) | copy-start | bytes 9220
  2126.1 357.0 %copy-start.117 = (f32[3072]{0:T(1024)S(1)}, f32[3072]{0:T(1024)}, u32[]{:S(2)}) copy-start(f32[3072]{0:T(1024)} %get-tuple-element.2634) | copy-start | bytes 36868
  2126.1 357.8 %copy-start.119 = (f32[2304]{0:T(1024)S(1)}, f32[2304]{0:T(1024)}, u32[]{:S(2)}) copy-start(f32[2304]{0:T(1024)} %copy-done.118) | copy-start | bytes 27652
  2126.1 487.8 %all-gather.7.cloned.1.call-start = ((), (), s32[]{:S(2)}) async-start(), calls=%async_computation.7 | async-start | bytes 1253376 | tf_op jit(solution)/shard_map/all_gather | solution.py:490
  2149.0 467.7 %all-gather.5.cloned.1.call-start = ((), (), s32[]{:S(2)}) async-start(), calls=%async_computation.5 | async-start | bytes 3760128 | tf_op jit(solution)/shard_map/all_gather | solution.py:490
  2243.4 378.9 %all-gather.11.cloned.1.call-start = ((), (), s32[]{:S(2)}) async-start(), calls=%async_computation.11 | async-start | bytes 5013504 | tf_op jit(solution)/shard_map/all_gather | solution.py:490
  2359.1 314.0 %all-gather.9.cloned.1.call-start = ((), (), s32[]{:S(2)}) async-start(), calls=%async_computation.9 | async-start | bytes 5013504 | tf_op jit(solution)/shard_map/all_gather | solution.py:490
  (268 other events, 1706.4 us)
Sparse Core Ops, SparseCore 0:
  2084.5 62.8 reduce-scatter.6
  2152.5 89.0 reduce-scatter.4
  2246.3 110.8 reduce-scatter.10
  2362.3 111.0 reduce-scatter.8
  2476.1 38.2 all-gather.6
  2517.2 46.2 all-gather.4
  2565.7 52.3 all-gather.10
  2621.0 52.0 all-gather.8
where the time goes:
time: 2710 us; the launch traced here: 2690 us
  waiting for transfers between devices  1040 us (38%)
  matrix products  702 us (26%)
  local copies, waits for them, and re-layouts  493 us (18%)
  other arithmetic  273 us (10%)
  blocking collectives  120 us (4%)
  loops' own time  27.3 us (1%)
    ppermute x4, waiting for transfers between devices, passed_along(): return lax.ppermute(array, axis, pairs)  658 us
    reduce_scatter x4, waiting for transfers between devices, shards(): lax.psum_scatter(accumulated, 'dp', scatter_dimension=0, tiled=True)  342 us
    dot_general x16, matrix products, product(): return jnp.dot(operand, matrix, preferred_element_type=jnp.float32)  122 us
    unnamed x2, blocking collectives  120 us
    dynamic_slice x64, local copies, waits for them, and re-layouts, attention(): lax.scan(jax.checkpoint(block_step), initial, (split_blocks(queries), spl...  103 us
    dot_general x64, matrix products, block_step(): jnp.einsum('bjhe,bjhf->bhef', key_sine, value_block, precision=PRECISE)  96.5 us
    squeeze x80, local copies, waits for them, and re-layouts, attention(): lax.scan(jax.checkpoint(block_step), initial, (split_blocks(queries), spl...  92 us
    dot_general x64, matrix products, block_step(): jnp.einsum('bjhe,bjhf->bhef', key_cosine, value_block, precision=PRECISE)  84.3 us
  transfers between devices with their start and end apart: 12, of which 8 were waited for; matrix products, arithmetic and copies ran while one was open for 4% of the time, Pallas kernels for 0%

commit v1 on v0

v1 whole, which is shorter than its diff:
```python
from functools import partial
import math

import jax
import jax.numpy as jnp
import numpy as np
from jax import lax
from jax.experimental import pallas as pl
from jax.experimental.pallas import tpu as pltpu
from jax.sharding import PartitionSpec as P

HEAD = 64
SEQ = 512
CHUNK = 256
PAIR = 2 * HEAD
EPSILON = 1e-05
MESH = pl.DeviceIdType.MESH
F32 = jnp.float32
BF16 = jnp.bfloat16
VMEM_BYTES = 63 * 2**20


def dot(a, b):
    return jnp.dot(a, b, preferred_element_type=F32)


def dot_nt(a, b):
    return lax.dot_general(a, b, (((1,), (1,)), ((), ())), preferred_element_type=F32)


def dot_tn(a, b):
    return lax.dot_general(a, b, (((0,), (0,)), ((), ())), preferred_element_type=F32)


def softplus(p):
    return jnp.maximum(p, 0.0) + jnp.log1p(jnp.exp(-jnp.abs(p)))


def sigmoid_of_softplus(q):
    series = q * (1.0 - q * (0.5 - q * (1.0 / 6.0 - q * (1.0 / 24.0))))
    return jnp.where(q < 0.03, series, 1.0 - jnp.exp(-q))


def cosine_tables():
    step = math.pi / (2.0 * SEQ)
    i = np.arange(CHUNK)[:, None]
    j = np.arange(CHUNK)[None, :]
    near = np.where(i >= j, np.cos((i - j) * step), 0.0).astype(np.float32)
    far = np.cos((i - j + CHUNK) * step).astype(np.float32)
    return near, far


def lane_masks():
    lanes = np.arange(PAIR)
    return np.stack([lanes < HEAD, lanes >= HEAD])[:, None, :].astype(np.float32)


def layer_kernel(
    boundary, inward, outward, expand, shrink,
    inbias, outbias, normgain, normshift, expbias, shrbias, lastgain, lastshift,
    near, far, masks,
    results, f_x, f_a, f_h, f_g, f_p, f_o, f_u, f_f, vectors,
    win, wout, wexp, wshr,
    xs, qkv, att, low, zin, hbs, gs, gps, n1s, n2s, s1s, s2s, dys, ybuf, xbuf,
    acc, keep, das, carry,
    load_sems, out_sems, res_sems, fwd_send, fwd_recv, bwd_send, bwd_recv,
):
    rows_all, width = xs.shape
    hidden = wexp.shape[1]
    chunks = rows_all // CHUNK
    pairs = width // PAIR
    slabs = hidden // width
    section = lax.axis_index("section")
    first = section == 0
    peer = {"section": 1 - section}

    loads = [
        pltpu.make_async_copy(src, dst, load_sems.at[i])
        for i, (src, dst) in enumerate(
            [(inward, win), (outward, wout), (expand, wexp), (shrink, wshr)]
        )
    ]
    load_x = pltpu.make_async_copy(boundary, xs, load_sems.at[4])
    load_y = pltpu.make_async_copy(boundary, dys, load_sems.at[4])

    @pl.when(first)
    def _():
        load_x.start()

    for load in loads:
        load.start()

    @pl.when(jnp.logical_not(first))
    def _():
        load_y.start()

    barrier = pltpu.get_barrier_semaphore()
    pl.semaphore_signal(barrier, inc=1, device_id=peer, device_id_type=MESH)
    vectors[...] = jnp.zeros_like(vectors)
    pl.semaphore_wait(barrier, 1)

    def rows_of(c):
        return pl.ds(pl.multiple_of(c * CHUNK, CHUNK), CHUNK)

    def send_forward(c):
        return pltpu.make_async_remote_copy(
            src_ref=ybuf.at[rows_of(c)], dst_ref=xs.at[rows_of(c)],
            send_sem=fwd_send.at[c], recv_sem=fwd_recv.at[c],
            device_id=peer, device_id_type=MESH,
        )

    def send_backward(c):
        return pltpu.make_async_remote_copy(
            src_ref=xbuf.at[rows_of(c)], dst_ref=dys.at[rows_of(c)],
            send_sem=bwd_send.at[c], recv_sem=bwd_recv.at[c],
            device_id=peer, device_id_type=MESH,
        )

    def result_copy(buf, c):
        return pltpu.make_async_copy(buf.at[rows_of(c)], results.at[rows_of(c)], res_sems.at[c])

    early = [(xs, f_x), (att, f_a), (hbs, f_h), (gs, f_g)]
    late = [(qkv, f_p), (n1s, f_o), (gps, f_u), (n2s, f_f)]

    def factor_copies(c, which, base):
        return [
            pltpu.make_async_copy(src.at[rows_of(c)], dst.at[rows_of(c)], out_sems.at[c, base + i])
            for i, (src, dst) in enumerate(which)
        ]

    def column_sum(at, value):
        vectors[at] += jnp.sum(value, axis=0, keepdims=True)

    def norm_forward(e):
        mean = jnp.mean(e, axis=-1, keepdims=True)
        center = e - mean
        s = lax.rsqrt(jnp.mean(center * center, axis=-1, keepdims=True) + EPSILON)
        return center * s, s

    def norm_backward(dn, n, s):
        m1 = jnp.mean(dn, axis=-1, keepdims=True)
        m2 = jnp.mean(dn * n, axis=-1, keepdims=True)
        return s * (dn - m1 - n * m2)

    def pair_columns(hp):
        return [pl.ds(pl.multiple_of(i * width + hp * PAIR, PAIR), PAIR) for i in range(3)]

    def attend(c, wide):
        rows = rows_of(c)
        tiles = [(rows, near)] + ([(rows_of(c - 1), far)] if wide else [])
        m = [masks[a].astype(BF16) for a in range(2)]

        def one_pair(hp, _):
            cq, ck, cv = pair_columns(hp)
            q = qkv[rows, cq]
            nz = None
            for key_rows, weights in tiles:
                k, v = qkv[key_rows, ck], qkv[key_rows, cv]
                for a in range(2):
                    s = (dot_nt(q * m[a], k) * weights[...]).astype(BF16)
                    right = jnp.concatenate(
                        [v * m[a], jnp.broadcast_to(m[a], v.shape)], axis=1
                    )
                    part = dot(s, right)
                    nz = part if nz is None else nz + part
            inverse = 1.0 / nz[:, PAIR:]
            a_full = nz[:, :PAIR] * inverse
            a_high = a_full.astype(BF16)
            att[rows, cq] = a_high
            low[rows, cq] = (a_full - a_high.astype(F32)).astype(BF16)
            zin[rows, cq] = inverse.astype(BF16)
            return 0

        lax.fori_loop(0, pairs, one_pair, 0)

    def attend_backward(c, wide):
        rows = rows_of(c)
        m = [masks[a].astype(BF16) for a in range(2)]

        def one_pair(hp, _):
            cq, ck, cv = pair_columns(hp)
            q, k, v = qkv[rows, cq], qkv[rows, ck], qkv[rows, cv]
            dn = (das[:, cq].astype(F32) * zin[rows, cq].astype(F32)).astype(BF16)
            prod = dn.astype(F32) * (att[rows, cq].astype(F32) + low[rows, cq].astype(F32))
            dz = [-jnp.sum(prod * masks[a], axis=-1, keepdims=True) for a in range(2)]
            qm = [q * m[a] for a in range(2)]
            dnm = [dn * m[a] for a in range(2)]

            def tile(kt, vt, weights):
                dq = dk = dv = None
                for a in range(2):
                    w = weights[...]
                    s = (dot_nt(qm[a], kt) * w).astype(BF16)
                    ds = ((dot_nt(dnm[a], vt) + dz[a]) * w).astype(BF16)
                    parts = (dot(ds, kt * m[a]), dot_tn(ds, qm[a]), dot_tn(s, dnm[a]))
                    dq, dk, dv = parts if a == 0 else (
                        dq + parts[0], dk + parts[1], dv + parts[2]
                    )
                return dq, dk, dv

            dq, dk, dv = tile(k, v, near)
            wide_cols = [pl.ds(pl.multiple_of(i * width + hp * PAIR, PAIR), PAIR) for i in range(2)]
            if wide:
                kp, vp = qkv[rows_of(c - 1), ck], qkv[rows_of(c - 1), cv]
                dqp, dkp, dvp = tile(kp, vp, far)
                dq = dq + dqp
                carry[:, wide_cols[0]] = dkp
                carry[:, wide_cols[1]] = dvp
            else:
                dk = dk + carry[:, wide_cols[0]]
                dv = dv + carry[:, wide_cols[1]]
            qkv[rows, cq] = (dq * sigmoid_of_softplus(q.astype(F32))).astype(BF16)
            qkv[rows, ck] = (dk * sigmoid_of_softplus(k.astype(F32))).astype(BF16)
            qkv[rows, cv] = dv.astype(BF16)
            return 0

        lax.fori_loop(0, pairs, one_pair, 0)

    def forward(c, begins):
        rows = rows_of(c)

        @pl.when(begins)
        def _():
            loads[0].wait()

            @pl.when(first)
            def _():
                load_x.wait()

        @pl.when(jnp.logical_not(first))
        def _():
            send_forward(c).wait_recv()

        for i in range(3):
            cols = slice(i * width, (i + 1) * width)
            p = dot(xs[rows, :], win[:, cols]) + inbias[:, cols]
            qkv[rows, cols] = (softplus(p) if i < 2 else p).astype(BF16)

        @pl.when(c % 2 == 0)
        def _():
            attend(c, False)

        @pl.when(c % 2 == 1)
        def _():
            attend(c, True)

        @pl.when(begins)
        def _():
            for load in loads[1:]:
                load.wait()

        e = xs[rows, :].astype(F32) + (dot(att[rows, :], wout[...]) + outbias[...])
        n1, s1 = norm_forward(e)
        n1s[rows, :] = n1.astype(BF16)
        s1s[rows, :] = s1
        h = n1 * normgain[...] + normshift[...]
        hbs[rows, :] = h.astype(BF16)
        acc[...] = h + shrbias[...]
        for i in range(slabs):
            cols = slice(i * width, (i + 1) * width)
            u = dot(hbs[rows, :], wexp[:, cols]) + expbias[:, cols]
            phi = 0.5 * (1.0 + lax.erf(u * math.sqrt(0.5)))
            g = (u * phi).astype(BF16)
            gs[rows, cols] = g
            gps[rows, cols] = (
                phi + u * (jnp.exp(u * u * -0.5) * (1.0 / math.sqrt(2.0 * math.pi)))
            ).astype(BF16)
            acc[...] += dot(g, wshr[cols, :])
        n2, s2 = norm_forward(acc[...])
        n2s[rows, :] = n2.astype(BF16)
        s2s[rows, :] = s2
        ybuf[rows, :] = (n2 * lastgain[...] + lastshift[...]).astype(BF16)

        @pl.when(first)
        def _():
            send_forward(c).start()

        @pl.when(jnp.logical_not(first))
        def _():
            result_copy(ybuf, c).start()

        for copy in factor_copies(c, early, 0):
            copy.start()

    def backward(c):
        rows = rows_of(c)

        @pl.when(first)
        def _():
            send_backward(c).wait_recv()

        @pl.when(jnp.logical_and(jnp.logical_not(first), c == 1))
        def _():
            load_y.wait()

        dy = dys[rows, :].astype(F32)
        n2 = n2s[rows, :].astype(F32)
        column_sum(7 + slabs, dy * n2)
        column_sum(8 + slabs, dy)
        dr = norm_backward(dy * lastgain[...], n2, s2s[rows, :])
        df = dr.astype(BF16)
        n2s[rows, :] = df
        column_sum(6 + slabs, df.astype(F32))
        acc[...] = dr
        for i in range(slabs):
            cols = slice(i * width, (i + 1) * width)
            dg = dot_nt(n2s[rows, :], wshr[cols, :])
            du = (dg * gps[rows, cols].astype(F32)).astype(BF16)
            gps[rows, cols] = du
            column_sum(6 + i, du.astype(F32))
            acc[...] += dot_nt(du, wexp[:, cols])
        dh = acc[...]
        n1 = n1s[rows, :].astype(F32)
        column_sum(4, dh * n1)
        column_sum(5, dh)
        de = norm_backward(dh * normgain[...], n1, s1s[rows, :])
        keep[...] = de
        do = de.astype(BF16)
        n1s[rows, :] = do
        column_sum(3, do.astype(F32))
        das[...] = dot_nt(do, wout[...]).astype(BF16)

        @pl.when(c % 2 == 0)
        def _():
            attend_backward(c, False)

        @pl.when(c % 2 == 1)
        def _():
            attend_backward(c, True)

        for i in range(3):
            column_sum(i, qkv[rows, i * width : (i + 1) * width].astype(F32))
        dx = keep[...] + dot_nt(qkv[rows, :], win[...])
        xbuf[rows, :] = dx.astype(BF16)

        @pl.when(first)
        def _():
            result_copy(xbuf, c).start()

        @pl.when(jnp.logical_not(first))
        def _():
            send_backward(c).start()

        for copy in factor_copies(c, late, 4):
            copy.start()

    def step(t, _):
        group, place = t // 4, t % 4
        ahead = jnp.where(first, t < chunks, place < 2)
        c_forward = jnp.where(first, t, 2 * group + place)
        back = t - chunks
        c_backward = jnp.where(first, 2 * (back // 2) + 1 - back % 2, 2 * group + 3 - place)

        @pl.when(ahead)
        def _():
            forward(c_forward, t == 0)

        @pl.when(jnp.logical_not(ahead))
        def _():
            backward(c_backward)

        return 0

    lax.fori_loop(0, 2 * chunks, step, 0)

    def finish(c, _):
        @pl.when(first)
        def _():
            send_forward(c).wait_send()
            result_copy(xbuf, c).wait()

        @pl.when(jnp.logical_not(first))
        def _():
            send_backward(c).wait_send()
            result_copy(ybuf, c).wait()

        for copy in factor_copies(c, early, 0) + factor_copies(c, late, 4):
            copy.wait()
        return 0

    lax.fori_loop(0, chunks, finish, 0)


def run_layer(boundary, weights, biases):
    rows, width = boundary.shape
    hidden = weights[2].shape[1]
    chunks = rows // CHUNK
    near, far = cosine_tables()
    masks = lane_masks()
    slabs = hidden // width
    any_space = pl.BlockSpec(memory_space=pl.ANY)
    vmem = pl.BlockSpec(memory_space=pltpu.VMEM)
    out_widths = [width] * 4 + [hidden, 3 * width, width, hidden, width]
    out_shape = [jax.ShapeDtypeStruct((rows, w), BF16) for w in out_widths]
    out_shape.append(jax.ShapeDtypeStruct((9 + slabs, 1, width), F32))
    low = lambda *shape: pltpu.VMEM(shape, BF16)
    wide = lambda *shape: pltpu.VMEM(shape, F32)
    dma = pltpu.SemaphoreType.DMA
    return pl.pallas_call(
        layer_kernel,
        out_shape=out_shape,
        in_specs=[any_space] * 5 + [vmem] * 11,
        out_specs=[any_space] * 9 + [vmem],
        scratch_shapes=[
            low(width, 3 * width), low(width, width), low(width, hidden), low(hidden, width),
            low(rows, width), low(rows, 3 * width), low(rows, width), low(rows, width),
            low(rows, width), low(rows, width), low(rows, hidden), low(rows, hidden),
            low(rows, width), low(rows, width), wide(rows, 1), wide(rows, 1),
            low(rows, width), low(rows, width), low(rows, width),
            wide(CHUNK, width), wide(CHUNK, width), low(CHUNK, width), wide(CHUNK, 2 * width),
            dma((5,)), dma((chunks, 8)), dma((chunks,)), dma((chunks,)), dma((chunks,)),
            dma((chunks,)), dma((chunks,)),
        ],
        compiler_params=pltpu.CompilerParams(
            collective_id=0, has_side_effects=True, vmem_limit_bytes=VMEM_BYTES
        ),
        name="layer",
    )(boundary, *weights, *biases, jnp.asarray(near), jnp.asarray(far), jnp.asarray(masks))


def shards(
    boundary, inward, inbias, outward, outbias, normgain, normshift, expand, expbias,
    shrink, shrbias, lastgain, lastshift,
):
    width = outward.shape[-1]
    hidden = expand.shape[-1]
    slabs = hidden // width
    outs = run_layer(
        boundary[0],
        (inward[0], outward[0], expand[0], shrink[0]),
        (inbias, outbias, normgain, normshift, expbias, shrbias, lastgain, lastshift),
    )
    results, f_x, f_a, f_h, f_g, f_p, f_o, f_u, f_f, vectors = outs

    def summed(left, right):
        grad = dot_tn(left, right).astype(BF16)
        mine = lax.psum_scatter(grad, "dp", scatter_dimension=0, tiled=True)
        return lax.all_gather(mine, "dp", axis=0, tiled=True).astype(F32)[None]

    vec = lax.psum(vectors.reshape(-1), "dp")

    def piece(start, count):
        return vec[start * width : (start + count) * width][None]

    return (
        results[None],
        summed(f_x, f_p), piece(0, 3),
        summed(f_a, f_o), piece(3, 1), piece(4, 1), piece(5, 1),
        summed(f_h, f_u), piece(6, slabs),
        summed(f_g, f_f), piece(6 + slabs, 1), piece(7 + slabs, 1), piece(8 + slabs, 1),
    )


def solution(mesh):
    matrix, vector = P("section", None, None), P("section", None)
    params = (
        matrix, vector, matrix, vector, vector, vector, matrix, vector, matrix, vector,
        vector, vector,
    )
    specs = (P("section", "dp", None),) + params
    return jax.shard_map(shards, mesh=mesh, in_specs=specs, out_specs=specs, check_vma=False)
```

time: 2710 us -> 641 us (0.24)
  matrix products: 702 us -> 31.4 us
  waiting for transfers between devices: 1040 us -> 377 us
  local copies, waits for them, and re-layouts: 493 us -> 8.56 us
  other arithmetic: 273 us -> 22.6 us
  Pallas kernels: 0 us -> 128 us
  blocking collectives: 120 us -> 58.3 us
  loops' own time: 27.3 us -> 0 us
    dot_general x512 -> x4, matrix products: 702 us -> 31.4 us  [dot_tn(): lax.dot_general(a, b, (((0,), (0,)), ((), ())), preferred_element_type=F32)]
    ppermute x4 -> x0, waiting for transfers between devices: 658 us -> none  [passed_along(): return lax.ppermute(array, axis, pairs)]
    pallas_call x0 -> x1, Pallas kernels: none -> 128 us  [run_layer(): pl.pallas_call(layer_kernel, out_shape=out_shape, in_specs=[any_space] *...]
    unnamed x2 -> x0, blocking collectives: 120 us -> none
    squeeze x86 -> x0, local copies, waits for them, and re-layouts: 107 us -> none  [the longest x80 92 us: attention(): lax.scan(jax.checkpoint(block_step), initial, (split_blocks(queries), spl...]
    dynamic_slice x64 -> x0, local copies, waits for them, and re-layouts: 103 us -> none  [attention(): lax.scan(jax.checkpoint(block_step), initial, (split_blocks(queries), spl...]
    reduce_scatter x4, waiting for transfers between devices: 342 us -> 259 us  [summed(): mine = lax.psum_scatter(grad, 'dp', scatter_dimension=0, tiled=True)]
    all_gather x4, waiting for transfers between devices: 44 us -> 118 us  [summed(): return lax.all_gather(mine, 'dp', axis=0, tiled=True).astype(F32)[None]]
  transfers between devices with their start and end apart: 12 -> 8, of which waited for: 8 -> 7; matrix products, arithmetic and copies ran while one was open for 4% -> 7% of each run, Pallas kernels for 0% -> 0%
where the time goes in v1:
time: 641 us
  waiting for transfers between devices  377 us (59%)
  Pallas kernels  128 us (20%)
  blocking collectives  58.3 us (9%)
  matrix products  31.4 us (5%)
  other arithmetic  22.6 us (4%)
  between operations  14.2 us (2%)
  local copies, waits for them, and re-layouts  8.56 us (1%)
    reduce_scatter x4, waiting for transfers between devices, summed(): mine = lax.psum_scatter(grad, 'dp', scatter_dimension=0, tiled=True)  259 us
    pallas_call x1, Pallas kernels, run_layer(): pl.pallas_call(layer_kernel, out_shape=out_shape, in_specs=[any_space] *...  128 us
    all_gather x4, waiting for transfers between devices, summed(): return lax.all_gather(mine, 'dp', axis=0, tiled=True).astype(F32)[None]  118 us
    psum x1, blocking collectives, shards(): vec = lax.psum(vectors.reshape(-1), 'dp')  58.3 us
    dot_general x4, matrix products, dot_tn(): lax.dot_general(a, b, (((0,), (0,)), ((), ())), preferred_element_type=F32)  31.4 us
    broadcast_in_dim x4, other arithmetic, summed(): return lax.all_gather(mine, 'dp', axis=0, tiled=True).astype(F32)[None]  22.5 us
  transfers between devices with their start and end apart: 8, of which 7 were waited for; matrix products, arithmetic and copies ran while one was open for 7% of the time, Pallas kernels for 0%

profile of v1, /device:TPU:0, one launch (start us, length us, event | category | flops | bytes accessed | tf_op | source)
XLA Modules:
  0.0 640.6 jit_solution(3091712493852656517)
XLA Ops:
  7.2 128.2 %layer.1 = (bf16[1024,768]{1,0:T(8,128)(2,1)}, bf16[1024,768]{1,0:T(8,128)(2,1)}, bf16[1024,768]{1,0:T(8,128)(2,1)}, bf16[1024,768]{1,0:T(8,128)(2,1)}, bf16[102...) custom-call(bf16[1024,768]{1,0:T(8,128)(2,1)} %bitcast.30, ...), custom_call_target="tpu_custom_call" | custom-call | tf_op jit(solution)/shard_map/layer/pallas_call | solution.py:399
  135.4 4.5 convolution_convert_fusion.3
  140.0 7.7 %convolution_convert_fusion.2 = bf16[768,2304]{1,0:T(8,128)(2,1)} fusion(bf16[1024,768]{1,0:T(8,128)(2,1)S(1)} %copy-done.4, bf16[1024,2304]{1,0:T(8,128)(2,1)} %get-tuple-element.25), kind=kOutput, calls=%fused_computation.2 | convolution fusion | flops 3625648128 | bytes 9830400 | tf_op jit(solution)/shard_map/dot_general | solution.py:32
  147.7 1.4 copy-done.3
  149.0 9.6 %convolution_convert_fusion.1 = bf16[768,3072]{1,0:T(8,128)(2,1)} fusion(bf16[1024,768]{1,0:T(8,128)(2,1)S(1)} %copy-done.3, bf16[1024,3072]{1,0:T(8,128)(2,1)} %get-tuple-element.30), kind=kOutput, calls=%fused_computation.1 | convolution fusion | flops 4834197504 | bytes 12582912 | tf_op jit(solution)/shard_map/dot_general | solution.py:32
  158.8 1.3 copy-done.2
  160.1 9.6 %convolution_convert_fusion = bf16[3072,768]{1,0:T(8,128)(2,1)} fusion(bf16[1024,3072]{1,0:T(8,128)(2,1)} %get-tuple-element.31, bf16[1024,768]{1,0:T(8,128)(2,1)S(1)} %copy-done.2), kind=kOutput, calls=%fused_computation | convolution fusion | flops 4834197504 | bytes 12582912 | tf_op jit(solution)/shard_map/dot_general | solution.py:32
  169.8 29.2 %reduce-scatter.7.cloned.1.call-done = bf16[48,768]{1,0:T(8,128)(2,1)} async-done(((bf16[768,768]{1,0:T(8,128)(2,1)}), bf16[48,768]{1,0:T(8,128)(2,1)}) %reduce-scatter.7.cloned.1.call-update) | async-done | bytes 73744 | tf_op jit(solution)/shard_map/reduce_scatter | solution.py:437
  199.1 71.4 %reduce-scatter.5.cloned.1.call-done = bf16[48,2304]{1,0:T(8,128)(2,1)} async-done(((bf16[768,2304]{1,0:T(8,128)(2,1)}), bf16[48,2304]{1,0:T(8,128)(2,1)}) %reduce-scatter.5.cloned.1.call-update) | async-done | bytes 221200 | tf_op jit(solution)/shard_map/reduce_scatter | solution.py:437
  270.6 78.8 %reduce-scatter.9.cloned.1.call-done = bf16[48,3072]{1,0:T(8,128)(2,1)} async-done(((bf16[768,3072]{1,0:T(8,128)(2,1)}), bf16[48,3072]{1,0:T(8,128)(2,1)}) %reduce-scatter.9.cloned.1.call-update) | async-done | bytes 294928 | tf_op jit(solution)/shard_map/reduce_scatter | solution.py:437
  349.5 79.4 %reduce-scatter.11.cloned.1.call-done = bf16[192,768]{1,0:T(8,128)(2,1)} async-done(((bf16[3072,768]{1,0:T(8,128)(2,1)}), bf16[192,768]{1,0:T(8,128)(2,1)}) %reduce-scatter.11.cloned.1.call-update) | async-done | bytes 294928 | tf_op jit(solution)/shard_map/reduce_scatter | solution.py:437
  429.0 58.3 %psum.7 = f32[9984]{0:T(1024)S(1)} all-reduce(f32[9984]{0:T(1024)S(1)} %reshape.29), channel_id=1, replica_groups=mesh['section'=2,'dp'=16] {'dp'}, use_global_device_ids=true, to_apply=%region_1.0 | all-reduce | flops 9984 | bytes 79872 | tf_op jit(solution)/shard_map/psum | solution.py:440
  487.3 0.6 slice.36
  487.9 0.6 broadcast_in_dim.54
  488.5 0.6 broadcast_in_dim.67
  489.1 0.6 broadcast_in_dim.66
  492.0 2.8 bitcast_convert_fusion.3
  494.9 22.0 %all-gather.5.cloned.1.call-done = bf16[768,2304]{1,0:T(8,128)(2,1)} async-done(((bf16[48,2304]{1,0:T(8,128)(2,1)}), bf16[768,2304]{1,0:T(8,128)(2,1)}) %all-gather.5.cloned.1.call-update) | async-done | bytes 3538960 | tf_op jit(solution)/shard_map/all_gather | solution.py:438
  516.9 5.5 bitcast_convert_fusion.2
  522.4 49.2 %all-gather.9.cloned.1.call-done = bf16[768,3072]{1,0:T(8,128)(2,1)} async-done(((bf16[48,3072]{1,0:T(8,128)(2,1)}), bf16[768,3072]{1,0:T(8,128)(2,1)}) %all-gather.9.cloned.1.call-update) | async-done | bytes 4718608 | tf_op jit(solution)/shard_map/all_gather | solution.py:438
  571.6 7.4 %bitcast_convert_fusion.1 = f32[1,768,3072]{2,1,0:T(8,128)} fusion(bf16[768,3072]{1,0:T(8,128)(2,1)} %all-gather.9.cloned.1.call-done), kind=kLoop, calls=%fused_computation.4 | loop fusion | flops 2359296 | bytes 14155776 | tf_op jit(solution)/shard_map/broadcast_in_dim | solution.py:438
  579.0 46.9 %all-gather.11.cloned.1.call-done = bf16[3072,768]{1,0:T(8,128)(2,1)} async-done(((bf16[192,768]{1,0:T(8,128)(2,1)}), bf16[3072,768]{1,0:T(8,128)(2,1)}) %all-gather.11.cloned.1.call-update) | async-done | bytes 4718608 | tf_op jit(solution)/shard_map/all_gather | solution.py:438
  625.8 6.8 %bitcast_convert_fusion = f32[1,3072,768]{2,1,0:T(8,128)} fusion(bf16[3072,768]{1,0:T(8,128)(2,1)} %all-gather.11.cloned.1.call-done), kind=kLoop, calls=%fused_computation.3 | loop fusion | flops 2359296 | bytes 14155776 | tf_op jit(solution)/shard_map/broadcast_in_dim | solution.py:438
  632.7 1.1 copy.30
  (33 shorter events, 2.9 us)
Async XLA Ops:
  7.2 191.9 %reduce-scatter.7.cloned.1.call-start = ((), (), s32[]{:S(2)}) async-start(), calls=%async_computation.6 | async-start | bytes 1253376 | tf_op jit(solution)/shard_map/reduce_scatter | solution.py:437
  135.4 4.5 copy-start.4
  139.9 130.6 %reduce-scatter.5.cloned.1.call-start = ((), (), s32[]{:S(2)}) async-start(), calls=%async_computation.4 | async-start | bytes 3760128 | tf_op jit(solution)/shard_map/reduce_scatter | solution.py:437
  147.6 1.4 copy-start.3
  147.6 201.8 %reduce-scatter.9.cloned.1.call-start = ((), (), s32[]{:S(2)}) async-start(), calls=%async_computation.8 | async-start | bytes 5013504 | tf_op jit(solution)/shard_map/reduce_scatter | solution.py:437
  158.7 1.4 copy-start.2
  158.7 270.2 %reduce-scatter.11.cloned.1.call-start = ((), (), s32[]{:S(2)}) async-start(), calls=%async_computation.10 | async-start | bytes 5013504 | tf_op jit(solution)/shard_map/reduce_scatter | solution.py:437
  169.8 259.2 %copy-start.1 = (f32[13,1,768]{2,1,0:T(1,128)S(1)}, f32[13,1,768]{2,1,0:T(1,128)}, u32[]{:S(2)}) copy-start(f32[13,1,768]{2,1,0:T(1,128)} %get-tuple-element.26) | copy-start | bytes 119812
  169.8 322.2 %all-gather.7.cloned.1.call-start = ((), (), s32[]{:S(2)}) async-start(), calls=%async_computation.7 | async-start | bytes 1253376 | tf_op jit(solution)/shard_map/all_gather | solution.py:438
  199.1 317.8 %all-gather.5.cloned.1.call-start = ((), (), s32[]{:S(2)}) async-start(), calls=%async_computation.5 | async-start | bytes 3760128 | tf_op jit(solution)/shard_map/all_gather | solution.py:438
  270.6 301.0 %all-gather.9.cloned.1.call-start = ((), (), s32[]{:S(2)}) async-start(), calls=%async_computation.9 | async-start | bytes 5013504 | tf_op jit(solution)/shard_map/all_gather | solution.py:438
  349.4 276.4 %all-gather.11.cloned.1.call-start = ((), (), s32[]{:S(2)}) async-start(), calls=%async_computation.11 | async-start | bytes 5013504 | tf_op jit(solution)/shard_map/all_gather | solution.py:438
  579.0 53.7 %copy-start = (bf16[1024,768]{1,0:T(8,128)(2,1)S(1)}, bf16[1024,768]{1,0:T(8,128)(2,1)}, u32[]{:S(2)}) copy-start(bf16[1024,768]{1,0:T(8,128)(2,1)} %get-tuple-element.23) | copy-start | bytes 4718596
Sparse Core Ops, SparseCore 0:
  140.0 59.0 reduce-scatter.6
  203.5 66.9 reduce-scatter.4
  275.0 74.3 reduce-scatter.8
  354.2 74.6 reduce-scatter.10
  431.0 37.6 all-gather.6
  470.9 45.9 all-gather.4
  519.2 52.3 all-gather.8
  573.9 51.9 all-gather.10

commit v2 on v1

--- a/solution.py
+++ b/solution.py
@@ -59,10 +59,10 @@
     boundary, inward, outward, expand, shrink,
     inbias, outbias, normgain, normshift, expbias, shrbias, lastgain, lastshift,
     near, far, masks,
-    results, f_x, f_a, f_h, f_g, f_p, f_o, f_u, f_f, vectors,
+    results, f_x, f_a, f_h, f_g, f_p, f_o, f_u, f_f, vector_rows,
     win, wout, wexp, wshr,
     xs, qkv, att, low, zin, hbs, gs, gps, n1s, n2s, s1s, s2s, dys, ybuf, xbuf,
-    acc, keep, das, carry,
+    acc, keep, das, carry, vectors,
     load_sems, out_sems, res_sems, fwd_send, fwd_recv, bwd_send, bwd_recv,
 ):
     rows_all, width = xs.shape
@@ -362,6 +362,8 @@
         return 0
 
     lax.fori_loop(0, 2 * chunks, step, 0)
+    for i in range(vectors.shape[0]):
+        vector_rows[i : i + 1, :] = vectors[i]
 
     def finish(c, _):
         @pl.when(first)
@@ -392,7 +394,8 @@
     vmem = pl.BlockSpec(memory_space=pltpu.VMEM)
     out_widths = [width] * 4 + [hidden, 3 * width, width, hidden, width]
     out_shape = [jax.ShapeDtypeStruct((rows, w), BF16) for w in out_widths]
-    out_shape.append(jax.ShapeDtypeStruct((9 + slabs, 1, width), F32))
+    vector_count = -(-(9 + slabs) // 8) * 8
+    out_shape.append(jax.ShapeDtypeStruct((vector_count, width), F32))
     low = lambda *shape: pltpu.VMEM(shape, BF16)
     wide = lambda *shape: pltpu.VMEM(shape, F32)
     dma = pltpu.SemaphoreType.DMA
@@ -408,6 +411,7 @@
             low(rows, width), low(rows, width), wide(rows, 1), wide(rows, 1),
             low(rows, width), low(rows, width), low(rows, width),
             wide(CHUNK, width), wide(CHUNK, width), low(CHUNK, width), wide(CHUNK, 2 * width),
+            wide(vector_count, 1, width),
             dma((5,)), dma((chunks, 8)), dma((chunks,)), dma((chunks,)), dma((chunks,)),
             dma((chunks,)), dma((chunks,)),
         ],
@@ -416,6 +420,355 @@
         ),
         name="layer",
     )(boundary, *weights, *biases, jnp.asarray(near), jnp.asarray(far), jnp.asarray(masks))
+
+
+SETS = 2
+LANES_Z = 4
+HOP_LAG = 2
+
+
+def gradient_kernel(
+    f_x, f_a, f_h, f_g, f_p, f_o, f_u, f_f, vec_in,
+    total, vec_out,
+    x, a, h, g, p, o, u, f,
+    part, core_in, chain_pair, chain_one, y_in, end_in, vec, vec_got,
+    load_sems, core_s, core_r, y_s, y_r, pair_s, pair_r, one_s, one_r, end_s, end_r,
+    got, z_s, yy_s, kept, out_s, out_r, vec_s, vec_r,
+):
+    width = x.shape[1]
+    slabs = g.shape[1] // width
+    me = lax.axis_index("dp")
+    core, y, z = me % 2, (me // 2) % 2, me // 4
+    last = LANES_Z - 1
+    core_peer, y_peer = {"dp": me + 1 - 2 * core}, {"dp": me + 2 - 4 * y}
+    hop = [last - z, z]
+    ahead = [{"dp": me - 4}, {"dp": me + 4}]
+    behind = [ahead[1], ahead[0]]
+
+    blocks = (
+        [(g, i, f, 0) for i in range(slabs)]
+        + [(h, 0, u, i) for i in range(slabs)]
+        + [(a, 0, o, 0)]
+        + [(x, 0, p, i) for i in range(3)]
+    )
+    duos = len(blocks) // 2
+    sets = duos * SETS
+    set_rows = width // SETS
+    half = set_rows // 2
+    piece = half // 4
+
+    sources = [(f_g, g), (f_f, f), (f_h, h), (f_u, u), (f_a, a), (f_o, o), (f_x, x), (f_p, p)]
+    loads = [
+        pltpu.make_async_copy(src, dst, load_sems.at[i]) for i, (src, dst) in enumerate(sources)
+    ]
+    load_at = {0: (0, 1), slabs // 2: (2, 3), slabs: (4, 5, 6, 7)}
+    for load in loads:
+        load.start()
+
+    barrier = pltpu.get_barrier_semaphore()
+    for peer in (core_peer, y_peer):
+        pl.semaphore_signal(barrier, inc=1, device_id=peer, device_id_type=MESH)
+    for d in range(2):
+        @pl.when(hop[d] < last)
+        def _():
+            pl.semaphore_signal(barrier, inc=1, device_id=ahead[d], device_id_type=MESH)
+    pl.semaphore_wait(barrier, jnp.where(jnp.logical_and(z > 0, z < last), 4, 3))
+
+    def remote(src, dst, send, recv, peer):
+        return pltpu.make_async_remote_copy(
+            src_ref=src, dst_ref=dst, send_sem=send, recv_sem=recv,
+            device_id=peer, device_id_type=MESH,
+        )
+
+    def span(k, d, first, count):
+        start = (k % SETS) * set_rows + d * half + first * piece
+        return pl.ds(pl.multiple_of(start, 16), count * piece)
+
+    def mine(k, d, first, count=1):
+        return part.at[k // SETS, core, span(k, d, first, count)]
+
+    def final(k, d, first, count=1):
+        return total.at[2 * (k // SETS) + core, span(k, d, first, count)]
+
+    def add(dst, src):
+        dst[...] = (dst[...].astype(F32) + src[...].astype(F32)).astype(BF16)
+
+    def core_copy(m):
+        return remote(part.at[m, 1 - core], core_in.at[m], core_s.at[m], core_r.at[m], core_peer)
+
+    def y_copy(k, d):
+        return remote(mine(k, d, 1 - y), y_in.at[k, d], y_s.at[k, d], y_r.at[k, d], y_peer)
+
+    def pair_copy(k, d):
+        return remote(
+            mine(k, d, 2, 2), chain_pair.at[k, d], pair_s.at[k, d], pair_r.at[k, d], ahead[d]
+        )
+
+    def one_copy(k, d):
+        return remote(mine(k, d, y), chain_one.at[k, d], one_s.at[k, d], one_r.at[k, d], ahead[d])
+
+    def end_copy(k, d):
+        return remote(mine(k, d, 3 - y), end_in.at[k], end_s.at[k], end_r.at[k], y_peer)
+
+    def spread_z(k, d, b, i, src):
+        return remote(src, final(k, d, b), z_s.at[k, d, i], got.at[k, d, b], behind[d])
+
+    def spread_y(k, d, b, i, src):
+        return remote(src, final(k, d, b), yy_s.at[k, d, i], got.at[k, d, b], y_peer)
+
+    def keep_copy(k, d, b, i):
+        return pltpu.make_async_copy(mine(k, d, b), final(k, d, b), kept.at[k, d, i])
+
+    def out_copy(k, d):
+        return remote(
+            final(k, d, 0, 4), final(k, d, 0, 4), out_s.at[k, d], out_r.at[k, d], core_peer
+        )
+
+    def arrived(k, d, b):
+        spread_z(k, d, b, 0, final(k, d, b)).wait_recv()
+
+    outer = jnp.logical_or(z == 0, z == last)
+    z_pair = {"dp": me + 4 - 8 * (z % 2)}
+    z_mid = {"dp": jnp.where(z == 1, me + 4, me - 4)}
+    z_out = {"dp": jnp.where(z == 1, me - 4, me + 4)}
+
+    def vec_copy(i, peer):
+        return remote(vec.at[i], vec_got.at[min(i, 3)], vec_s.at[i], vec_r.at[min(i, 3)], peer)
+
+    def compute(m):
+        for i in load_at.get(m, ()):
+            loads[i].wait()
+        for side in range(2):
+            left, i, right, j = blocks[2 * m + side]
+            for r in range(3):
+                rows = slice(r * (width // 3), (r + 1) * (width // 3))
+                cols = slice(i * width + rows.start, i * width + rows.stop)
+                part[m, side, rows, :] = dot_tn(
+                    left[:, cols], right[:, j * width : (j + 1) * width]
+                ).astype(BF16)
+        core_copy(m).start()
+
+    vec[0] = vec_in[...]
+    vec_copy(0, core_peer).start()
+    compute(0)
+
+    def tick(t, _):
+        for m in range(1, duos):
+            @pl.when(t == SETS * (m - 1))
+            def _():
+                compute(m)
+
+        for i, peer in ((1, y_peer), (2, z_pair)):
+            @pl.when(t == i)
+            def _():
+                vec_copy(i - 1, peer).wait_recv()
+                vec[i] = vec[i - 1] + vec_got[i - 1]
+                vec_copy(i, peer).start()
+
+        @pl.when(t == 3)
+        def _():
+            vec_copy(2, z_pair).wait_recv()
+            vec[3] = vec[2] + vec_got[2]
+
+            @pl.when(jnp.logical_not(outer))
+            def _():
+                vec_copy(3, z_mid).start()
+
+        @pl.when(jnp.logical_and(t == 4, jnp.logical_not(outer)))
+        def _():
+            vec_copy(3, z_mid).wait_recv()
+            vec[4] = vec[3] + vec_got[3]
+            vec_copy(4, z_out).start()
+            vec_out[...] = vec[4]
+
+        @pl.when(jnp.logical_and(t == 5, outer))
+        def _():
+            vec_copy(3, z_mid).wait_recv()
+            vec_out[...] = vec_got[3]
+
+        @pl.when(t < sets)
+        def _():
+            @pl.when(t % SETS == 0)
+            def _():
+                m = t // SETS
+                core_copy(m).wait_recv()
+                for r in range(3):
+                    rows = pl.ds(r * (width // 3), width // 3)
+                    add(part.at[m, core, rows], core_in.at[m, rows])
+
+            for d in range(2):
+                y_copy(t, d).start()
+
+                @pl.when(hop[d] == 0)
+                def _():
+                    pair_copy(t, d).start()
+
+        def during(k, more=True):
+            return jnp.logical_and(jnp.logical_and(k >= 0, k < sets), more)
+
+        k = t - 1
+
+        @pl.when(during(k))
+        def _():
+            for d in range(2):
+                y_copy(k, d).wait_recv()
+                add(mine(k, d, y), y_in.at[k, d])
+
+                @pl.when(hop[d] == 0)
+                def _():
+                    one_copy(k, d).start()
+
+        for d in range(2):
+            k = t - 1 - HOP_LAG * hop[d]
+
+            @pl.when(during(k, hop[d] > 0))
+            def _():
+                pair_copy(k, d).wait_recv()
+                add(mine(k, d, 2, 2), chain_pair.at[k, d])
+
+                @pl.when(hop[d] < last)
+                def _():
+                    pair_copy(k, d).start()
+
+                @pl.when(hop[d] == last)
+                def _():
+                    end_copy(k, d).start()
+
+                one_copy(k, d).wait_recv()
+                add(mine(k, d, y), chain_one.at[k, d])
+
+                @pl.when(hop[d] < last)
+                def _():
+                    one_copy(k, d).start()
+
+        base = 2 + HOP_LAG * last
+        for d in range(2):
+            k = t - base
+
+            @pl.when(during(k, hop[d] == last))
+            def _():
+                spread_z(k, d, y, 0, mine(k, d, y)).start()
+                spread_y(k, d, y, 0, mine(k, d, y)).start()
+                keep_copy(k, d, y, 0).start()
+                end_copy(k, d).wait_recv()
+                add(mine(k, d, 2 + y), end_in.at[k])
+                spread_y(k, d, 2 + y, 1, mine(k, d, 2 + y)).start()
+                spread_z(k, d, 2 + y, 1 + y, mine(k, d, 2 + y)).start()
+                keep_copy(k, d, 2 + y, 1).start()
+
+            k2 = t - base - 1
+
+            @pl.when(during(k2, hop[d] == last))
+            def _():
+                arrived(k2, d, 3 - y)
+                spread_z(k2, d, 3 - y, 2 - y, final(k2, d, 3 - y)).start()
+
+            k3 = t - base - HOP_LAG * (last - hop[d])
+
+            @pl.when(during(k3, hop[d] < last))
+            def _():
+                for i, b in ((0, y), (1, 2), (2, 3)):
+                    arrived(k3, d, b)
+
+                    @pl.when(hop[d] > 0)
+                    def _():
+                        spread_z(k3, d, b, i, final(k3, d, b)).start()
+
+                    if i == 0:
+                        spread_y(k3, d, b, 0, final(k3, d, b)).start()
+
+            k4 = k3 - 1
+
+            @pl.when(during(k4))
+            def _():
+                arrived(k4, d, 1 - y)
+
+                @pl.when(hop[d] == last)
+                def _():
+                    keep_copy(k4, d, y, 0).wait()
+                    keep_copy(k4, d, 2 + y, 1).wait()
+
+                out_copy(k4, d).start()
+
+        return 0
+
+    ticks = sets + 2 + HOP_LAG * last + HOP_LAG * last + 1
+    lax.fori_loop(0, ticks, tick, 0)
+
+    def settle(k, _):
+        for d in range(2):
+            y_copy(k, d).wait_send()
+            out_copy(k, d).wait()
+            spread_y(k, d, y, 0, final(k, d, y)).wait_send()
+
+            @pl.when(hop[d] < last)
+            def _():
+                pair_copy(k, d).wait_send()
+                one_copy(k, d).wait_send()
+
+            @pl.when(hop[d] == last)
+            def _():
+                end_copy(k, d).wait_send()
+                spread_y(k, d, 2 + y, 1, final(k, d, 2 + y)).wait_send()
+
+            @pl.when(hop[d] > 0)
+            def _():
+                for i, b in ((0, y), (1, 2), (2, 3)):
+                    spread_z(k, d, b, i, final(k, d, b)).wait_send()
+
+        return 0
+
+    lax.fori_loop(0, sets, settle, 0)
+
+    def settle_core(m, _):
+        core_copy(m).wait_send()
+        return 0
+
+    lax.fori_loop(0, duos, settle_core, 0)
+    for i in range(3):
+        vec_copy(i, core_peer).wait_send()
+
+    @pl.when(jnp.logical_not(outer))
+    def _():
+        vec_copy(3, z_mid).wait_send()
+        vec_copy(4, z_out).wait_send()
+
+
+def reduce_gradients(factors, vectors):
+    rows, width = factors[0].shape
+    hidden = factors[3].shape[1]
+    blocks = 4 + 2 * (hidden // width)
+    duos = blocks // 2
+    sets = duos * SETS
+    piece = width // SETS // 8
+    any_space = pl.BlockSpec(memory_space=pl.ANY)
+    vmem = pl.BlockSpec(memory_space=pltpu.VMEM)
+    low = lambda *shape: pltpu.VMEM(shape, BF16)
+    dma = lambda *shape: pltpu.SemaphoreType.DMA(shape)
+    return pl.pallas_call(
+        gradient_kernel,
+        out_shape=[
+            jax.ShapeDtypeStruct((blocks, width, width), BF16),
+            jax.ShapeDtypeStruct(vectors.shape, F32),
+        ],
+        in_specs=[any_space] * 8 + [vmem],
+        out_specs=[any_space, vmem],
+        scratch_shapes=[low(*factor.shape) for factor in factors]
+        + [
+            low(duos, 2, width, width), low(duos, width, width),
+            low(sets, 2, 2 * piece, width), low(sets, 2, piece, width),
+            low(sets, 2, piece, width), low(sets, piece, width),
+            pltpu.VMEM((5,) + vectors.shape, F32), pltpu.VMEM((4,) + vectors.shape, F32),
+            dma(8), dma(duos), dma(duos), dma(sets, 2), dma(sets, 2), dma(sets, 2), dma(sets, 2),
+            dma(sets, 2), dma(sets, 2), dma(sets), dma(sets),
+            dma(sets, 2, 4), dma(sets, 2, 3), dma(sets, 2, 2), dma(sets, 2, 2), dma(sets, 2),
+            dma(sets, 2), dma(5), dma(4),
+        ],
+        compiler_params=pltpu.CompilerParams(
+            collective_id=1, has_side_effects=True, vmem_limit_bytes=VMEM_BYTES
+        ),
+        name="gradients",
+    )(*factors, vectors)
 
 
 def shards(
@@ -430,24 +783,38 @@
         (inward[0], outward[0], expand[0], shrink[0]),
         (inbias, outbias, normgain, normshift, expbias, shrbias, lastgain, lastshift),
     )
-    results, f_x, f_a, f_h, f_g, f_p, f_o, f_u, f_f, vectors = outs
-
-    def summed(left, right):
-        grad = dot_tn(left, right).astype(BF16)
-        mine = lax.psum_scatter(grad, "dp", scatter_dimension=0, tiled=True)
-        return lax.all_gather(mine, "dp", axis=0, tiled=True).astype(F32)[None]
-
-    vec = lax.psum(vectors.reshape(-1), "dp")
+    results, factors, vectors = outs[0], outs[1:9], outs[9]
+    if lax.axis_size("dp") == 4 * LANES_Z:
+        total, vec = reduce_gradients(factors, vectors)
+
+        def beside(blocks):
+            return jnp.concatenate([block.astype(F32) for block in blocks], axis=1)
+
+        shrink_grad = total[:slabs].reshape(hidden, width).astype(F32)
+        expand_grad = beside([total[slabs + i] for i in range(slabs)])
+        outward_grad = total[2 * slabs].astype(F32)
+        inward_grad = beside([total[2 * slabs + 1 + i] for i in range(3)])
+    else:
+        f_x, f_a, f_h, f_g, f_p, f_o, f_u, f_f = factors
+
+        def summed(left, right):
+            grad = dot_tn(left, right).astype(BF16)
+            mine = lax.psum_scatter(grad, "dp", scatter_dimension=0, tiled=True)
+            return lax.all_gather(mine, "dp", axis=0, tiled=True).astype(F32)
+
+        inward_grad, outward_grad = summed(f_x, f_p), summed(f_a, f_o)
+        expand_grad, shrink_grad = summed(f_h, f_u), summed(f_g, f_f)
+        vec = lax.psum(vectors, "dp")
 
     def piece(start, count):
-        return vec[start * width : (start + count) * width][None]
+        return vec[start : start + count].reshape(1, count * width)
 
     return (
         results[None],
-        summed(f_x, f_p), piece(0, 3),
-        summed(f_a, f_o), piece(3, 1), piece(4, 1), piece(5, 1),
-        summed(f_h, f_u), piece(6, slabs),
-        summed(f_g, f_f), piece(6 + slabs, 1), piece(7 + slabs, 1), piece(8 + slabs, 1),
+        inward_grad[None], piece(0, 3),
+        outward_grad[None], piece(3, 1), piece(4, 1), piece(5, 1),
+        expand_grad[None], piece(6, slabs),
+        shrink_grad[None], piece(6 + slabs, 1), piece(7 + slabs, 1), piece(8 + slabs, 1),
     )
 
 

time: 641 us -> 328 us (0.51)
  waiting for transfers between devices: 377 us -> 0 us
  Pallas kernels: 128 us -> 301 us
  blocking collectives: 58.3 us -> 0 us
  matrix products: 31.4 us -> 0 us
  between operations: 14.2 us -> 0.68 us
    reduce_scatter x4 -> x0, waiting for transfers between devices: 259 us -> none  [summed(): mine = lax.psum_scatter(grad, 'dp', scatter_dimension=0, tiled=True)]
    pallas_call x0 -> x1, Pallas kernels: none -> 173 us  [reduce_gradients(): pl.pallas_call(gradient_kernel, out_shape=[jax.ShapeDtypeStruct((blocks,...]
    all_gather x4 -> x0, waiting for transfers between devices: 118 us -> none  [summed(): return lax.all_gather(mine, 'dp', axis=0, tiled=True).astype(F32)[None]]
    psum x1 -> x0, blocking collectives: 58.3 us -> none  [shards(): vec = lax.psum(vectors.reshape(-1), 'dp')]
    dot_general x4 -> x0, matrix products: 31.4 us -> none  [dot_tn(): lax.dot_general(a, b, (((0,), (0,)), ((), ())), preferred_element_type=F32)]
    broadcast_in_dim x4 -> x2, other arithmetic: 22.5 us -> 7.51 us  [the longest x1 4.32 us: shards(): expand_grad[None]]
    convert_element_type x0 -> x2, other arithmetic: none -> 9.74 us  [the longest x1 5.26 us: beside(): return jnp.concatenate([block.astype(F32) for block in blocks], axis=1)]
  transfers between devices with their start and end apart: 8 -> 0, of which waited for: 7 -> 0; matrix products, arithmetic and copies ran while one was open for 7% -> 0% of each run, Pallas kernels for 0% -> 0%
where the time goes in v2:
time: 328 us; the launch traced here: 327 us
  Pallas kernels  301 us (92%)
  other arithmetic  17.2 us (5%)
  local copies, waits for them, and re-layouts  8.04 us (2%)
    pallas_call x1, Pallas kernels, reduce_gradients(): pl.pallas_call(gradient_kernel, out_shape=[jax.ShapeDtypeStruct((blocks,...  173 us
    pallas_call x1, Pallas kernels, run_layer(): pl.pallas_call(layer_kernel, out_shape=out_shape, in_specs=[any_space] *...  128 us

profile of v2, /device:TPU:0, one launch (start us, length us, event | category | flops | bytes accessed | tf_op | source)
XLA Modules:
  0.0 327.5 jit_solution(637295653467596580)
XLA Ops:
  0.6 128.1 %layer.1 = (bf16[1024,768]{1,0:T(8,128)(2,1)}, bf16[1024,768]{1,0:T(8,128)(2,1)}, bf16[1024,768]{1,0:T(8,128)(2,1)}, bf16[1024,768]{1,0:T(8,128)(2,1)}, bf16[102...) custom-call(bf16[1024,768]{1,0:T(8,128)(2,1)} %bitcast.46, ...), custom_call_target="tpu_custom_call" | custom-call | tf_op jit(solution)/shard_map/layer/pallas_call | solution.py:402
  128.8 173.4 %gradients.1 = (bf16[12,768,768]{2,1,0:T(8,128)(2,1)}, f32[16,768]{1,0:T(8,128)}) custom-call(bf16[1024,768]{1,0:T(8,128)(2,1)} %get-tuple-element.26.f_x, bf16[1024,768]{1,0:T(8,128)(2,1)} %get-tuple-element.27.f_a, bf16[1024,768]{1,0:T(8,128)(2,1)} %get-tuple-element.28.f_h, bf16[1024,3072]{1,0:T(8,128)(2,1)} %get-tuple-element.29.f_g, ...), custom_call_target="tpu_custom_call" | custom-call | tf_op jit(solution)/shard_map/gradients/pallas_call | solution.py:748
  302.2 0.8 slice_bitcast_fusion.7
  303.0 0.6 copy.30
  303.6 0.7 slice_bitcast_fusion.8
  304.3 1.5 fusion.2
  305.8 0.6 copy.29
  306.4 2.6 slice.64
  309.1 5.3 %slice_bitcast_fusion.3 = (bf16[768,768]{1,0:T(8,128)(2,1)S(1)}, bf16[768,768]{1,0:T(8,128)(2,1)S(1)}, bf16[768,768]{1,0:T(8,128)(2,1)S(1)}, bf16[768,768]{1,0:T...) fusion(bf16[12,768,768]{2,1,0:T(8,128)(2,1)} %get-tuple-element.35), kind=kLoop, calls=%fused_computation.8 | loop fusion | flops 589824 | bytes 20054016 | tf_op jit(solution)/shard_map/convert_element_type | solution.py:791
  314.3 4.5 %bitcast_convert_fusion = f32[1,3072,768]{2,1,0:T(8,128)} fusion(bf16[1,3072,768]{2,1,0:T(8,128)(2,1)S(1)} %bitcast.42), kind=kLoop, calls=%fused_computation.2 | loop fusion | flops 2359296 | bytes 14155776 | tf_op jit(solution)/shard_map/convert_element_type | solution.py:793
  318.8 4.3 %fusion = f32[1,768,3072]{2,1,0:T(8,128)} fusion(bf16[768,768]{1,0:T(8,128)(2,1)S(1)} %get-tuple-element.38, bf16[768,768]{1,0:T(8,128)(2,1)S(1)} %get-tuple-element.39, bf16[768,768]{1,0:T(8,128)(2,1)S(1)} %get-tuple-element.40, bf16[768,768]{1,0:T(8,128)(2,1)S(1)} %get-tuple-element.37), kind=kLoop, calls=%fused_computation.1 | loop fusion | flops 21233664 | bytes 14155776 | tf_op jit(solution)/shard_map/broadcast_in_dim | solution.py:816
  323.1 0.0 copy-start
  323.1 3.2 fusion.1
  326.3 0.0 copy-done
  326.3 1.1 copy.32
Async XLA Ops:
  323.1 3.2 copy-start
